TPU v7x, 1024 devices: a whole 8x8x8 slice. The times are simulated.
1024 devices in a mesh: dp: 8 (over z), tensor: 2 (over core), expert: 64 (over x, y).
Axes of the slice: x: 8, y: 8, z: 8, core: 2. Of those that a mesh axis runs over, the one named last changes fastest.
Arguments:
- tokens: bfloat16 [8192, 4096], P('expert', 'dp'), may hold values from -6 to 6
- cotangent: bfloat16 [8192, 4096], P('expert', 'dp'), may hold values from -6 to 6
- routes: int32 [8192, 4], P('expert'), may hold values from 0 to 63, all different within a row; in each aligned block of 128 rows (0 to 127, 128 to 255, ...) at most 10 rows name the same one
- gates: bfloat16 [8192, 4], P('expert'), may hold values from 0.019897461 to 0.5
- w_gate: bfloat16 [64, 4096, 1536], P('expert', 'dp', 'tensor'), may hold values from -0.09375 to 0.09375
- w_up: bfloat16 [64, 4096, 1536], P('expert', 'dp', 'tensor'), may hold values from -0.09375 to 0.09375
- w_down: bfloat16 [64, 1536, 4096], P('expert', 'tensor', 'dp'), may hold values from -0.15625 to 0.15625
Outputs:
- input_grad: bfloat16 [8192, 4096], P('expert', 'dp')
- down_grad: bfloat16 [64, 1536, 4096], P('expert', 'tensor', 'dp')
Inputs may be any that keep to these rules, and one draw needn't show every extreme that they name: `routes`: each row names 4 different experts. In each aligned block of 128 rows (the rows of one device) no expert is named by more than 10 rows, a bound that some block reaches.
All inputs are finite; a program needn't handle non-finite values.
Results may differ from a plain program's by a relative error of at most 0.029.
Values may be sent and summed in bfloat16 or wider, within the bound.
A program may use at most 32 MiB of HBM per device.

v0:
```python
import jax
import jax.numpy as jnp
from jax import lax
from jax.sharding import PartitionSpec as P


def body(tokens, cotangent, routes, gates, w_gate, w_up, w_down):
    tok_dev, width_loc = tokens.shape
    top_count = routes.shape[1]
    experts = lax.axis_size("expert")
    groups = lax.axis_size("dp")
    capacity = max(2, 5 * tok_dev * top_count // (4 * experts))
    total_rows = experts * capacity
    share_rows = total_rows // groups
    pair_count = tok_dev * top_count
    route_flat = routes.reshape(pair_count)
    onehot = (route_flat[:, None] == jnp.arange(experts, dtype=jnp.int32)[None, :]).astype(
        jnp.int32
    )
    before = jnp.cumsum(onehot, axis=0) - onehot
    slot_rank = jnp.sum(before * onehot, axis=1)
    slot_index = route_flat * capacity + slot_rank
    slot_owner = (
        jnp.zeros((total_rows,), jnp.int32)
        .at[slot_index]
        .set(jnp.arange(1, pair_count + 1, dtype=jnp.int32))
    )
    token_row = jnp.where(slot_owner > 0, (slot_owner - 1) // top_count + 1, 0)
    zero_row = jnp.zeros((1, width_loc), tokens.dtype)
    send_x = jnp.concatenate([zero_row, tokens], 0)[token_row].reshape(experts, capacity, width_loc)
    send_dy = jnp.concatenate([zero_row, cotangent], 0)[token_row].reshape(
        experts, capacity, width_loc
    )
    gate_pad = jnp.concatenate([jnp.zeros((1,), gates.dtype), gates.reshape(pair_count)], 0)
    send_g = gate_pad[slot_owner].reshape(experts, capacity)
    recv_x, recv_dy, recv_g = (
        lax.all_to_all(send_x, "expert", split_axis=0, concat_axis=0, tiled=True),
        lax.all_to_all(send_dy, "expert", split_axis=0, concat_axis=0, tiled=True),
        lax.all_to_all(send_g, "expert", split_axis=0, concat_axis=0, tiled=True),
    )
    x_rows = recv_x.reshape(total_rows, width_loc)
    dy_rows = recv_dy.reshape(total_rows, width_loc)
    weight_rows = recv_g.reshape(total_rows).astype(jnp.float32)
    gate_proj = w_gate[0]
    up_proj = w_up[0]
    down_proj = w_down[0]
    hidden_loc = gate_proj.shape[1]
    dy_block = dy_rows
    gate_part = jnp.dot(x_rows, gate_proj, preferred_element_type=jnp.float32)
    up_part = jnp.dot(x_rows, up_proj, preferred_element_type=jnp.float32)
    back_part = lax.dot_general(
        dy_block, down_proj, (((1,), (1,)), ((), ())), preferred_element_type=jnp.float32
    )
    partials = lax.psum_scatter(
        jnp.concatenate([gate_part, up_part, back_part], axis=1).astype(jnp.bfloat16),
        "dp",
        scatter_dimension=0,
        tiled=True,
    ).astype(jnp.float32)
    gate_sum = partials[:, :hidden_loc]
    up_sum = partials[:, hidden_loc : 2 * hidden_loc]
    back_sum = partials[:, 2 * hidden_loc :]
    weight_share = lax.dynamic_slice_in_dim(
        weight_rows, lax.axis_index("dp") * share_rows, share_rows, 0
    )
    sig_gate = jax.nn.sigmoid(gate_sum)
    silu_val = gate_sum * sig_gate
    d_hidden = weight_share[:, None] * back_sum
    d_up = (d_hidden * silu_val).astype(jnp.bfloat16)
    d_gate = (d_hidden * up_sum * sig_gate * (1.0 + gate_sum * (1.0 - sig_gate))).astype(
        jnp.bfloat16
    )
    scaled = (weight_share[:, None] * silu_val * up_sum).astype(jnp.bfloat16)
    piece_gate = lax.all_gather(d_gate, "dp", axis=0, tiled=True)
    piece_up = lax.all_gather(d_up, "dp", axis=0, tiled=True)
    piece_scaled = lax.all_gather(scaled, "dp", axis=0, tiled=True)
    dx_piece = lax.dot_general(
        piece_gate, gate_proj, (((1,), (1,)), ((), ())), preferred_element_type=jnp.float32
    )
    dx_piece = dx_piece + lax.dot_general(
        piece_up, up_proj, (((1,), (1,)), ((), ())), preferred_element_type=jnp.float32
    )
    dy_block = dy_rows
    down_acc = lax.dot_general(
        piece_scaled, dy_block, (((0,), (0,)), ((), ())), preferred_element_type=jnp.float32
    )
    dx_rows, down_acc = (dx_piece, down_acc)
    summed = lax.psum(dx_rows.astype(jnp.bfloat16), "tensor").astype(jnp.float32)
    cols = summed.shape[1]
    moved = lax.all_to_all(
        summed.reshape(experts, capacity, cols).astype(jnp.bfloat16),
        "expert",
        split_axis=0,
        concat_axis=0,
        tiled=True,
    ).astype(jnp.float32)
    row_grads = moved.reshape(total_rows, cols)
    combine_cols = row_grads.shape[1]
    result = jnp.sum(
        row_grads[slot_index].reshape(tok_dev, top_count, combine_cols), axis=1
    ).astype(jnp.bfloat16)
    return (result, down_acc.astype(jnp.bfloat16)[None])


def solution(mesh):
    return jax.shard_map(
        body,
        mesh=mesh,
        in_specs=(
            P("expert", "dp"),
            P("expert", "dp"),
            P("expert", None),
            P("expert", None),
            P("expert", "dp", "tensor"),
            P("expert", "dp", "tensor"),
            P("expert", "tensor", "dp"),
        ),
        out_specs=(P("expert", "dp"), P("expert", "tensor", "dp")),
        check_vma=False,
    )
```

profile of v0, /device:TPU:14, one launch (start us, length us, event | category | flops | bytes accessed | tf_op | source)
XLA Modules:
  0.0 310.6 jit_solution(10732657335457438341)
XLA Ops:
  7.2 0.8 broadcast_multiply_fusion
  7.9 0.8 copy.16
  9.2 1.2 reduce-window.6
  10.8 2.4 scatter_custom_fusion
  13.3 0.9 concatenate.14
  14.2 2.8 gather_fusion.1
  17.1 1.2 reshape.87
  18.3 17.5 %all-to-all-start.1 = ((bf16[64,10,512]{2,1,0:T(8,128)(2,1)}), bf16[64,10,512]{2,1,0:T(8,128)(2,1)S(1)}, u32[]{:S(2)}, u32[]{:S(2)}) async-start(bf16[64,10,512]{2,1,0:T(8,128)(2,1)} %reshape.87), calls=%async_computation.1 | async-start | bytes 2097152 | tf_op jit(solution)/shard_map/all_to_all | solution.py:37
  35.8 2.8 gather_fusion.2
  38.6 1.2 reshape.89
  39.8 20.9 %all-to-all-done.1 = bf16[64,10,512]{2,1,0:T(8,128)(2,1)S(1)} async-done(((bf16[64,10,512]{2,1,0:T(8,128)(2,1)}), bf16[64,10,512]{2,1,0:T(8,128)(2,1)S(1)}, u32[]{:S(2)}, u32[]{:S(2)}) %all-to-all-start.1) | async-done | bytes 655392 | tf_op jit(solution)/shard_map/all_to_all | solution.py:37
  60.7 7.6 %all-to-all-start.2 = ((bf16[64,10,512]{2,1,0:T(8,128)(2,1)}), bf16[64,10,512]{2,1,0:T(8,128)(2,1)S(1)}, u32[]{:S(2)}, u32[]{:S(2)}) async-start(bf16[64,10,512]{2,1,0:T(8,128)(2,1)} %reshape.89), calls=%async_computation.2 | async-start | bytes 2097152 | tf_op jit(solution)/shard_map/all_to_all | solution.py:38
  68.6 1.8 convolution_convert_fusion.1
  70.4 1.7 convolution_convert_fusion.2
  72.1 24.2 %all-to-all-done.2 = bf16[64,10,512]{2,1,0:T(8,128)(2,1)S(1)} async-done(((bf16[64,10,512]{2,1,0:T(8,128)(2,1)}), bf16[64,10,512]{2,1,0:T(8,128)(2,1)S(1)}, u32[]{:S(2)}, u32[]{:S(2)}) %all-to-all-start.2) | async-done | bytes 655392 | tf_op jit(solution)/shard_map/all_to_all | solution.py:38
  96.5 1.9 convolution_convert_fusion
  98.5 1.8 pad_maximum_fusion
  101.3 4.3 %gather_fusion = bf16[640]{0:T(1024)(128)(2,1)S(1)} fusion(bf16[513]{0:T(1024)(128)(2,1)S(1)} %pad_maximum_fusion.1, s32[1024]{0:T(1024)S(1)} %get-tuple-element.8), kind=kCustom, calls=%fused_computation | custom fusion | bytes 5120 | tf_op jit(solution)/shard_map/gather | solution.py:35
  105.6 0.8 all_to_all.20
  106.3 7.5 %all-to-all-start = ((bf16[64,1,10]{2,1,0:T(2,128)(2,1)}), bf16[64,1,10]{2,1,0:T(2,128)(2,1)S(1)}, u32[]{:S(2)}, u32[]{:S(2)}) async-start(bf16[64,1,10]{2,1,0:T(2,128)(2,1)} %all_to_all.20), calls=%async_computation | async-start | bytes 65536 | tf_op jit(solution)/shard_map/all_to_all | solution.py:39
  114.0 9.3 %all-to-all-done = bf16[64,1,10]{2,1,0:T(2,128)(2,1)S(1)} async-done(((bf16[64,1,10]{2,1,0:T(2,128)(2,1)}), bf16[64,1,10]{2,1,0:T(2,128)(2,1)S(1)}, u32[]{:S(2)}, u32[]{:S(2)}) %all-to-all-start) | async-done | bytes 1312 | tf_op jit(solution)/shard_map/all_to_all | solution.py:39
  123.6 34.7 %reduce-scatter.2.cloned.1.call-done = bf16[80,2304]{1,0:T(8,128)(2,1)} async-done(((bf16[640,2304]{1,0:T(8,128)(2,1)}), bf16[80,2304]{1,0:T(8,128)(2,1)}) %reduce-scatter.2.cloned.1.call-update) | async-done | bytes 368656 | tf_op jit(solution)/shard_map/reduce_scatter | solution.py:54
  158.2 1.0 convert_element_type.45
  159.5 26.9 %all_gather.9 = bf16[640,768]{1,0:T(8,128)(2,1)S(1)} all-gather(bf16[80,768]{1,0:T(8,128)(2,1)S(1)} %get-tuple-element.3), channel_id=1, replica_groups=mesh['dp'=8,'tensor'=2,'expert'=64] {'dp'}, dimensions={0}, use_global_device_ids=true | all-gather | bytes 1105920 | tf_op jit(solution)/shard_map/all_gather | solution.py:74
  187.0 26.5 %all_gather.10 = bf16[640,768]{1,0:T(8,128)(2,1)S(1)} all-gather(bf16[80,768]{1,0:T(8,128)(2,1)S(1)} %get-tuple-element.4), channel_id=1, replica_groups=mesh['dp'=8,'tensor'=2,'expert'=64] {'dp'}, dimensions={0}, use_global_device_ids=true | all-gather | bytes 1105920 | tf_op jit(solution)/shard_map/all_gather | solution.py:75
  214.2 1.2 convert_element_type.49
  215.5 40.3 %all-reduce.4.cloned.1.call-done = bf16[64,10,512]{2,1,0:T(8,128)(2,1)} async-done(((bf16[64,10,512]{2,1,0:T(8,128)(2,1)}), bf16[64,10,512]{2,1,0:T(8,128)(2,1)}) %all-reduce.4.cloned.1.call-update) | async-done | bytes 655376 | tf_op jit(solution)/shard_map/psum | solution.py:88
  255.8 13.2 %all-to-all-start.3 = ((bf16[64,10,512]{2,1,0:T(8,128)(2,1)}), bf16[64,10,512]{2,1,0:T(8,128)(2,1)S(1)}, u32[]{:S(2)}, u32[]{:S(2)}) async-start(bf16[64,10,512]{2,1,0:T(8,128)(2,1)} %all-reduce.4.cloned.1.call-done), calls=%async_computation.4 | async-start | bytes 2097152 | tf_op jit(solution)/shard_map/all_to_all | solution.py:90
  269.0 29.6 %all_gather.11 = bf16[640,768]{1,0:T(8,128)(2,1)S(1)} all-gather(bf16[80,768]{1,0:T(8,128)(2,1)S(1)} %get-tuple-element.2), channel_id=1, replica_groups=mesh['dp'=8,'tensor'=2,'expert'=64] {'dp'}, dimensions={0}, use_global_device_ids=true | all-gather | bytes 1105920 | tf_op jit(solution)/shard_map/all_gather | solution.py:76
  298.6 1.7 fusion.1
  300.5 1.6 gather_fusion.3
  302.5 1.3 reduce_sum.22
  (43 shorter events, 4.9 us)
Async XLA Ops:
  7.2 63.2 %copy-start = (bf16[1,512,768]{2,1,0:T(8,128)(2,1)S(1)}, bf16[1,512,768]{2,1,0:T(8,128)(2,1)}, u32[]{:S(2)}) copy-start(bf16[1,512,768]{2,1,0:T(8,128)(2,1)} %param.11) | copy-start | bytes 2359300
  17.0 18.7 %copy-start.3 = (bf16[128,512]{1,0:T(8,128)(2,1)S(1)}, bf16[128,512]{1,0:T(8,128)(2,1)}, u32[]{:S(2)}) copy-start(bf16[128,512]{1,0:T(8,128)(2,1)} %param.8) | copy-start | bytes 393220
  18.3 42.4 %all-to-all-start.1 = ((bf16[64,10,512]{2,1,0:T(8,128)(2,1)}), bf16[64,10,512]{2,1,0:T(8,128)(2,1)S(1)}, u32[]{:S(2)}, u32[]{:S(2)}) async-start(bf16[64,10,512]{2,1,0:T(8,128)(2,1)} %reshape.87), calls=%async_computation.1 | async-start | bytes 2097152 | tf_op jit(solution)/shard_map/all_to_all | solution.py:37
  60.7 35.6 %all-to-all-start.2 = ((bf16[64,10,512]{2,1,0:T(8,128)(2,1)}), bf16[64,10,512]{2,1,0:T(8,128)(2,1)S(1)}, u32[]{:S(2)}, u32[]{:S(2)}) async-start(bf16[64,10,512]{2,1,0:T(8,128)(2,1)} %reshape.89), calls=%async_computation.2 | async-start | bytes 2097152 | tf_op jit(solution)/shard_map/all_to_all | solution.py:38
  68.3 89.9 %reduce-scatter.2.cloned.1.call-start = ((), (), s32[]{:S(2)}) async-start(), calls=%async_computation.5 | async-start | bytes 3317760 | tf_op jit(solution)/shard_map/reduce_scatter | solution.py:54
  96.5 1.9 copy-start.1
  100.2 0.7 copy-start.4
  106.3 16.9 %all-to-all-start = ((bf16[64,1,10]{2,1,0:T(2,128)(2,1)}), bf16[64,1,10]{2,1,0:T(2,128)(2,1)S(1)}, u32[]{:S(2)}, u32[]{:S(2)}) async-start(bf16[64,1,10]{2,1,0:T(2,128)(2,1)} %all_to_all.20), calls=%async_computation | async-start | bytes 65536 | tf_op jit(solution)/shard_map/all_to_all | solution.py:39
  113.9 141.9 %all-reduce.4.cloned.1.call-start = ((), (), s32[]{:S(2)}) async-start(), calls=%async_computation.6 | async-start | bytes 2097152 | tf_op jit(solution)/shard_map/psum | solution.py:88
  186.3 27.2 %copy-start.2 = (bf16[1,512,768]{2,1,0:T(8,128)(2,1)S(1)}, bf16[1,512,768]{2,1,0:T(8,128)(2,1)}, u32[]{:S(2)}) copy-start(bf16[1,512,768]{2,1,0:T(8,128)(2,1)} %param.12) | copy-start | bytes 2359300
  255.8 44.5 %all-to-all-start.3 = ((bf16[64,10,512]{2,1,0:T(8,128)(2,1)}), bf16[64,10,512]{2,1,0:T(8,128)(2,1)S(1)}, u32[]{:S(2)}, u32[]{:S(2)}) async-start(bf16[64,10,512]{2,1,0:T(8,128)(2,1)} %all-reduce.4.cloned.1.call-done), calls=%async_computation.4 | async-start | bytes 2097152 | tf_op jit(solution)/shard_map/all_to_all | solution.py:90
Sparse Core Ops, SparseCore 0:
  100.4 57.8 reduce-scatter.1
  215.6 40.1 all-reduce.3
where the time goes:
time: 311 us
  waiting for transfers between devices  129 us (41%)
  blocking collectives  83 us (27%)
  starting transfers between devices  45.9 us (15%)
  local copies, waits for them, and re-layouts  22.9 us (7%)
  between operations  14.3 us (5%)
  matrix products  8.49 us (3%)
  other arithmetic  6.65 us (2%)
    psum x1, waiting for transfers between devices, body(): lax.psum(dx_rows.astype(jnp.bfloat16), 'tensor').astype(jnp.float32)  40.3 us
    reduce_scatter x1, waiting for transfers between devices, body(): lax.psum_scatter(jnp.concatenate([gate_part, up_part, back_part], axis=1)...  34.7 us
    all_gather x1, blocking collectives, body(): piece_scaled = lax.all_gather(scaled, 'dp', axis=0, tiled=True)  29.6 us
    all_gather x1, blocking collectives, body(): piece_gate = lax.all_gather(d_gate, 'dp', axis=0, tiled=True)  26.9 us
    all_gather x1, blocking collectives, body(): piece_up = lax.all_gather(d_up, 'dp', axis=0, tiled=True)  26.5 us
    all_to_all x1, waiting for transfers between devices, body(): lax.all_to_all(send_dy, 'expert', split_axis=0, concat_axis=0, tiled=True)  24.2 us
    all_to_all x1, waiting for transfers between devices, body(): lax.all_to_all(send_x, 'expert', split_axis=0, concat_axis=0, tiled=True)  20.9 us
    all_to_all x1, starting transfers between devices, body(): lax.all_to_all(send_x, 'expert', split_axis=0, concat_axis=0, tiled=True)  17.5 us
  transfers between devices with their start and end apart: 6, of which 5 were waited for; matrix products, arithmetic and copies ran while one was open for 5% of the time, Pallas kernels for 0%

commit v1 on v0

v1 whole, which is shorter than its diff:
```python
import functools
import math

import jax
import jax.numpy as jnp
from jax import lax
from jax.experimental import pallas as pl
from jax.experimental.pallas import tpu as pltpu
from jax.sharding import PartitionSpec as P

MESH = pl.DeviceIdType.MESH
F32 = jnp.float32
BF16 = jnp.bfloat16


def dot(a, b, dims=((1,), (0,))):
    return lax.dot_general(a, b, (dims, ((), ())), preferred_element_type=F32)


def kernel(
    c,
    routes_ref, gates_ref, tok_ref, cot_ref, wg_hbm, wu_hbm, wd_hbm,
    dx_ref, dgrad_ref,
    wg, wu, wd, perm, fin, pcomb,
    s1, a1, s2, a2, rows, own, st0, rs, gat, keep, pxo, pxi, rt, ra, r2, rc, res,
    wsem, d1s, d1r, d2s, d2r, cxs, cxr, rss, rsr, ags, agr, pxs, pxr, r1s, r1r, r2s, r2r, fs, fr,
):
    n, nz, cap, tok, top, width, hid = c
    half_z = nz // 2
    total = n * n * cap
    chunk = total // nz
    block = n * cap
    per = nz // n
    hw = width // 2
    hh = hid // 2
    order = [r for pair in zip(range(n // 2, 0, -1), range(n - n // 2, n)) for r in pair]
    order = list(dict.fromkeys(r for r in order if 0 < r < n))

    z = lax.axis_index("dp")
    core = lax.axis_index("tensor")
    me = lax.axis_index("expert")
    mx, my = me // n, lax.rem(me, n)
    first = (1 - core) * mx + core * my
    second = (1 - core) * my + core * mx

    def at_x(p):
        return {"expert": p * n + my}

    def at_y(p):
        return {"expert": mx * n + p}

    def at_first(p):
        return {"expert": (1 - core) * (p * n + my) + core * (mx * n + p)}

    def at_second(p):
        return {"expert": (1 - core) * (mx * n + p) + core * (p * n + my)}

    other = {"tensor": 1 - core}
    z_to = ({"dp": lax.rem(z + 1, nz)}, {"dp": lax.rem(z + nz - 1, nz)})

    def z_off(k):
        return lax.rem(z + k + 2 * nz, nz)

    def span(i, size):
        return pl.ds(pl.multiple_of(i * size, size), size)

    mine = span(core, hw)
    theirs = span(1 - core, hw)

    loads = [
        pltpu.make_async_copy(src, dst, wsem.at[i])
        for i, (src, dst) in enumerate(((wg_hbm, wg), (wu_hbm, wu), (wd_hbm, wd)))
    ]
    for load in loads:
        load.start()

    barrier = pltpu.get_barrier_semaphore()
    peers = [at_x(lax.rem(mx + r, n)) for r in range(1, n)]
    peers += [at_y(lax.rem(my + r, n)) for r in range(1, n)]
    peers += [other, z_to[0], z_to[1]]
    for peer in peers:
        pl.semaphore_signal(barrier, inc=1, device_id=peer, device_id_type=MESH)

    ex = n * n
    e_row = lax.broadcasted_iota(jnp.int32, (ex, 1), 0).astype(F32)
    e_div = jnp.floor((e_row + 0.5) * (1.0 / n))
    e_swap = (e_row - e_div * n) * n + e_div
    core_f = core.astype(F32)
    e_disp = e_row + core_f * (e_swap - e_row)
    s_row = lax.broadcasted_iota(jnp.int32, (total, 1), 0).astype(F32)
    s_exp = jnp.floor((s_row + 0.5) * (1.0 / cap))
    s_rank = s_row - s_exp * cap
    expand = (s_exp == lax.broadcasted_iota(jnp.int32, (total, ex), 1).astype(F32)).astype(BF16)
    earlier = (
        lax.broadcasted_iota(jnp.int32, (tok, tok), 0) < lax.broadcasted_iota(jnp.int32, (tok, tok), 1)
    ).astype(BF16)
    routes = routes_ref[...].astype(F32)
    gates = gates_ref[...].astype(F32)

    def select(names):
        member = jnp.zeros((ex, tok), F32)
        weight = jnp.zeros((ex, tok), F32)
        for k in range(top):
            hit = routes[k : k + 1, :] == names
            member = member + jnp.where(hit, 1.0, 0.0)
            weight = weight + jnp.where(hit, gates[k : k + 1, :], 0.0)
        rank = dot(member.astype(BF16), earlier)
        placed = (member * (rank + 1.0)).astype(BF16)
        return dot(expand, placed) == s_rank + 1.0, weight

    picked, weight = select(e_disp)
    chosen = jnp.where(picked, 1.0, 0.0).astype(BF16)
    weighted = jnp.where(picked, dot(expand, weight.astype(BF16)), 0.0).astype(BF16)
    s1[0] = dot(chosen, tok_ref[:, mine]).astype(BF16)

    pl.semaphore_wait(barrier, len(peers))

    def exchange(src, dst, ssem, rsem, here, where):
        out = []
        for r in order:
            peer = lax.rem(here + r, n)
            out.append(
                pltpu.make_async_remote_copy(
                    src_ref=src.at[span(peer, block), :],
                    dst_ref=dst.at[span(here, block), :],
                    send_sem=ssem.at[r],
                    recv_sem=rsem.at[r],
                    device_id=where(peer),
                    device_id_type=MESH,
                )
            )
        return out

    pending = []

    def go(copies):
        for copy in copies:
            copy.start()
            pending.append(copy)

    d1 = [exchange(s1.at[i], a1.at[i], d1s.at[i], d1r.at[i], first, at_first) for i in range(2)]
    d2 = [exchange(s2.at[i], a2.at[i], d2s.at[i], d2r.at[i], second, at_second) for i in range(2)]

    go(d1[0])
    a1[0, span(first, block), :] = s1[0, span(first, block), :]
    s1[1] = dot(weighted, cot_ref[:, mine]).astype(BF16)
    go(d1[1])
    a1[1, span(first, block), :] = s1[1, span(first, block), :]

    s_a = jnp.floor((s_row + 0.5) * (1.0 / block))
    s_b = s_exp - s_a * n
    swapped = s_b * block + s_a * cap + s_rank
    lane = lax.broadcasted_iota(jnp.int32, (total, total), 1).astype(F32)
    perm[...] = jnp.where(lane == swapped, 1.0, 0.0).astype(BF16)
    last = s_row + core_f * (swapped - s_row)
    fin[...] = jnp.where(lane == last, 1.0, 0.0).astype(BF16)
    back_home, _ = select(e_row)
    pcomb[...] = jnp.where(back_home, 1.0, 0.0).astype(BF16)

    def stage_two(i):
        for copy in d1[i]:
            copy.wait_recv()
        s2[i] = dot(perm[...], a1[i]).astype(BF16)
        go(d2[i])
        a2[i, span(second, block), :] = s2[i, span(second, block), :]

    swap = [
        pltpu.make_async_remote_copy(
            src_ref=rows.at[i, :, mine],
            dst_ref=rows.at[i, :, mine],
            send_sem=cxs.at[i],
            recv_sem=cxr.at[i],
            device_id=other,
            device_id_type=MESH,
        )
        for i in range(2)
    ]

    def stage_three(i):
        for copy in d2[i]:
            copy.wait_recv()
        rows[i, :, mine] = dot(fin[...], a2[i]).astype(BF16)
        go([swap[i]])
        swap[i].wait_recv()

    tile = 256 if hid % 256 == 0 else hid

    def partial(j):
        loads[j].wait()

        def step(f, _):
            cols = span(f, tile)
            if j == 2:
                own[j, :, cols] = dot(rows[1], wd[cols, :], ((1,), (1,)))
            else:
                own[j, :, cols] = dot(rows[0], (wg, wu)[j][:, cols])
            return 0

        lax.fori_loop(0, hid // tile, step, 0)

    def cut(d):
        return slice(0, hh) if d == 0 else slice(hh, hid)

    def rs_copy(d, s, j):
        if s == 0:
            src, dst = st0.at[j, :, cut(d)], rs.at[d, 0, j, :, cut(d)]
        else:
            src, dst = rs.at[d, s - 1, j], rs.at[d, s, j]
        return pltpu.make_async_remote_copy(
            src_ref=src, dst_ref=dst, send_sem=rss.at[d, s, j], recv_sem=rsr.at[d, s, j],
            device_id=z_to[d], device_id_type=MESH,
        )

    ring = {(d, s, j): rs_copy(d, s, j) for d in range(2) for s in range(half_z) for j in range(3)}

    def rs_step(s, j):
        if s == 0:
            st0[j] = own[j, span(z_off(half_z), chunk), :].astype(BF16)
            go([ring[0, 0, j], ring[1, 0, j]])
            return
        for d in range(2):
            sign = 1 - 2 * d
            ring[d, s - 1, j].wait_recv()
            at = span(z_off(sign * (half_z - s)), chunk)
            if s == 1:
                a, b = cut(d), cut(1 - d)
                rs[d, 0, j, :, a] = (rs[d, 0, j, :, a].astype(F32) + own[j, at, a]).astype(BF16)
                rs[d, 0, j, :, b] = own[j, at, b].astype(BF16)
            else:
                rs[d, s - 1, j] = (rs[d, s - 1, j].astype(F32) + own[j, at, :]).astype(BF16)
            go([ring[d, s, j]])

    def rs_sum(j):
        ring[0, half_z - 1, j].wait_recv()
        ring[1, half_z - 1, j].wait_recv()
        return (
            own[j, span(z, chunk), :]
            + rs[0, half_z - 1, j].astype(F32)
            + rs[1, half_z - 1, j].astype(F32)
        )

    def ag_copy(d, s, j):
        at = span(z_off((2 * d - 1) * s), chunk)
        ref = gat.at[j, at, cut(d)] if s == half_z - 1 else gat.at[j, at, :]
        return pltpu.make_async_remote_copy(
            src_ref=ref, dst_ref=ref, send_sem=ags.at[d, s, j], recv_sem=agr.at[d, s, j],
            device_id=z_to[d], device_id_type=MESH,
        )

    def ag_arrived(d, s, j):
        at = span(z_off((2 * d - 1) * (s + 1)), chunk)
        ref = gat.at[j, at, cut(d)] if s == half_z - 1 else gat.at[j, at, :]
        pltpu.make_async_remote_copy(
            src_ref=ref, dst_ref=ref, send_sem=ags.at[d, s, j], recv_sem=agr.at[d, s, j],
            device_id=z_to[d], device_id_type=MESH,
        ).wait_recv()

    stage_two(0)
    stage_two(1)
    stage_three(0)
    partial(0)
    rs_step(0, 0)
    partial(1)
    rs_step(0, 1)
    rs_step(1, 0)
    rs_step(1, 1)
    stage_three(1)
    partial(2)
    rs_step(0, 2)
    for s in range(2, half_z):
        rs_step(s, 0)
        rs_step(s, 1)
        rs_step(s - 1, 2)
    rs_step(half_z - 1, 2)

    here = span(z, chunk)
    gate = rs_sum(0)
    sig = jax.nn.sigmoid(gate)
    silu = gate * sig
    up = rs_sum(1)
    gat[2, here, :] = (silu * up).astype(BF16)
    go([ag_copy(d, 0, 2) for d in range(2)])
    back = rs_sum(2)
    gat[0, here, :] = (back * up * sig * (1.0 + gate * (1.0 - sig))).astype(BF16)
    go([ag_copy(d, 0, 0) for d in range(2)])
    gat[1, here, :] = (back * silu).astype(BF16)
    go([ag_copy(d, 0, 1) for d in range(2)])

    def px_copy(k):
        return pltpu.make_async_remote_copy(
            src_ref=pxo.at[k], dst_ref=pxi.at[k], send_sem=pxs.at[k], recv_sem=pxr.at[k],
            device_id=other, device_id_type=MESH,
        )

    def grads(k):
        at = span(z_off(k), chunk)
        val = dot(gat[0, at, :], wg[...], ((1,), (1,))) + dot(gat[1, at, :], wu[...], ((1,), (1,)))
        keep[k] = val
        pxo[k] = keep[k, :, theirs].astype(BF16)
        go([px_copy(k)])

    def home_copy(k):
        at = z_off(k)
        peer = at // per
        sub = lax.rem(at, per)
        slot = lax.rem(peer + n - my, n) * per + sub
        return pltpu.make_async_remote_copy(
            src_ref=rt.at[k], dst_ref=ra.at[span(my * per + sub, chunk), :],
            send_sem=r1s.at[slot], recv_sem=r1r.at[slot],
            device_id=at_y(peer), device_id_type=MESH,
        )

    def settle(k):
        px_copy(k).wait_recv()
        val = (keep[k, :, mine] + pxi[k].astype(F32)).astype(BF16)
        rt[k] = val
        at = z_off(k)

        @pl.when(at // per == my)
        def _():
            ra[span(at, chunk), :] = val

        @pl.when(at // per != my)
        def _():
            home_copy(k).start()

    grads(0)
    done = [0]
    for s in range(1, half_z + 1):
        for j in (2, 0, 1):
            for d in range(2):
                ag_arrived(d, s - 1, j)
                if s < half_z:
                    go([ag_copy(d, s, j)])
        for k in done:
            settle(k)
        done = [s, nz - s] if s < half_z else [s]
        if s == half_z:
            grads(s)
        else:
            grads(s)
            grads(nz - s)
    ftile = 256 if hid % 256 == 0 else hid

    def down(f, _):
        cols = span(f, ftile)
        dgrad_ref[cols, :] = dot(gat[2, :, cols], rows[1], ((0,), (0,))).astype(BF16)
        return 0

    for k in done:
        settle(k)
    lax.fori_loop(0, hid // ftile, down, 0)

    for r in range(1, n):
        for sub in range(per):
            slot = r * per + sub
            pltpu.make_async_remote_copy(
                src_ref=rt.at[0],
                dst_ref=ra.at[span(lax.rem(my + n - r, n) * per + sub, chunk), :],
                send_sem=r1s.at[slot], recv_sem=r1r.at[slot],
                device_id=at_y(lax.rem(my + r, n)), device_id_type=MESH,
            ).wait_recv()
    r2[...] = dot(perm[...], ra[...]).astype(BF16)
    home = exchange(r2, rc, r2s, r2r, mx, at_x)
    go(home)
    rc[span(mx, block), :] = r2[span(mx, block), :]
    for copy in home:
        copy.wait_recv()
    res[:, mine] = dot(pcomb[...], rc[...], ((0,), (0,))).astype(BF16)
    last_swap = pltpu.make_async_remote_copy(
        src_ref=res.at[:, mine], dst_ref=res.at[:, mine], send_sem=fs.at[0], recv_sem=fr.at[0],
        device_id=other, device_id_type=MESH,
    )
    go([last_swap])
    last_swap.wait_recv()
    dx_ref[...] = res[...]

    for copy in pending:
        copy.wait_send()
    for k in range(nz):
        at = z_off(k)

        @pl.when(at // per != my)
        def _():
            home_copy(k).wait_send()


def body(tokens, cotangent, routes, gates, w_gate, w_up, w_down):
    tok, width = tokens.shape
    top = routes.shape[1]
    hid = w_gate.shape[2]
    experts = lax.axis_size("expert")
    nz = lax.axis_size("dp")
    n = math.isqrt(experts)
    cap = max(2, 5 * tok * top // (4 * experts))
    total = experts * cap
    chunk = total // nz
    hw = width // 2
    hz = nz // 2
    vm = pltpu.VMEM
    dma = pltpu.SemaphoreType.DMA
    in_vmem = pl.BlockSpec(memory_space=pltpu.VMEM)
    in_hbm = pl.BlockSpec(memory_space=pl.ANY)
    scratch = [
        vm((width, hid), BF16), vm((width, hid), BF16), vm((hid, width), BF16),
        vm((total, total), BF16), vm((total, total), BF16), vm((total, tok), BF16),
        vm((2, total, hw), BF16), vm((2, total, hw), BF16), vm((2, total, hw), BF16), vm((2, total, hw), BF16),
        vm((2, total, width), BF16),
        vm((3, total, hid), F32),
        vm((3, chunk, hid), BF16),
        vm((2, hz, 3, chunk, hid), BF16),
        vm((3, total, hid), BF16),
        vm((nz, chunk, width), F32),
        vm((nz, chunk, hw), BF16), vm((nz, chunk, hw), BF16), vm((nz, chunk, hw), BF16),
        vm((total, hw), BF16), vm((total, hw), BF16), vm((total, hw), BF16),
        vm((tok, width), BF16),
        dma((3,)),
        dma((2, n)), dma((2, n)), dma((2, n)), dma((2, n)),
        dma((2,)), dma((2,)),
        dma((2, hz, 3)), dma((2, hz, 3)), dma((2, hz, 3)), dma((2, hz, 3)),
        dma((nz,)), dma((nz,)),
        dma((nz,)), dma((nz,)),
        dma((n,)), dma((n,)),
        dma((1,)), dma((1,)),
    ]
    dx, dgrad = pl.pallas_call(
        functools.partial(kernel, (n, nz, cap, tok, top, width, hid)),
        out_shape=(
            jax.ShapeDtypeStruct((tok, width), BF16),
            jax.ShapeDtypeStruct((hid, width), BF16),
        ),
        in_specs=[in_vmem] * 4 + [in_hbm] * 3,
        out_specs=(in_vmem, in_vmem),
        scratch_shapes=scratch,
        compiler_params=pltpu.CompilerParams(
            collective_id=0, has_side_effects=True, vmem_limit_bytes=52 * 1024 * 1024
        ),
        cost_estimate=pl.CostEstimate(
            flops=12 * total * width * hid, bytes_accessed=8 * width * hid, transcendentals=chunk * hid
        ),
    )(routes.T, gates.T, tokens, cotangent, w_gate[0], w_up[0], w_down[0])
    return dx, dgrad[None]


def solution(mesh):
    return jax.shard_map(
        body,
        mesh=mesh,
        in_specs=(
            P("expert", "dp"),
            P("expert", "dp"),
            P("expert", None),
            P("expert", None),
            P("expert", "dp", "tensor"),
            P("expert", "dp", "tensor"),
            P("expert", "tensor", "dp"),
        ),
        out_specs=(P("expert", "dp"), P("expert", "tensor", "dp")),
        check_vma=False,
    )
```

time: 311 us -> 125 us (0.40)
  the two profiles are of different devices: /device:TPU:14 before, /device:TPU:65 now
where the time goes in v1:
time: 125 us
  Pallas kernels  119 us (95%)
  local copies, waits for them, and re-layouts  5.16 us (4%)
    pallas_call x1, Pallas kernels, body(): pl.pallas_call(functools.partial(kernel, (n, nz, cap, tok, top, width, hi...  119 us
    unnamed x12, local copies, waits for them, and re-layouts  5.16 us

profile of v1, /device:TPU:65, one launch (start us, length us, event | category | flops | bytes accessed | tf_op | source)
XLA Modules:
  0.0 125.0 jit_solution(5696823188923486816)
XLA Ops:
  0.6 0.0 copy-start.3
  0.6 0.0 copy-start.4
  0.7 0.7 copy-done.3
  1.3 0.0 copy-done.4
  1.3 0.0 copy-start
  1.3 1.1 copy-done
  2.5 0.0 copy-start.1
  2.5 0.9 copy-done.1
  3.4 0.0 copy-start.2
  3.4 0.9 copy-done.2
  4.3 119.2 %shard_map.86 = (bf16[128,512]{1,0:T(8,128)(2,1)S(1)}, bf16[768,512]{1,0:T(8,128)(2,1)S(1)}) custom-call(s32[4,128]{1,0:T(4,128)S(1)} %bitcast.8, bf16[4,128]{1,0:T(4,128)(2,1)S(1)} %bitcast.9, bf16[128,512]{1,0:T(8,128)(2,1)S(1)} %copy-done.1, bf16[128,512]{1,0:T(8,128)(2,1)S(1)} %copy-done.2, bf16[512,768]{1,0:T(8,128)(2,1)S(1)} %bitcast.7, ...), custom_call_target="tpu_custom_call" | custom-call | flops 3019898880 | bytes 3145728 | tf_op jit(solution)/shard_map/pallas_call | solution.py:426
  123.5 0.7 copy.11
  124.1 0.9 copy.12
Async XLA Ops:
  0.6 0.7 copy-start.3
  0.6 0.7 copy-start.4
  1.3 1.1 copy-start
  2.5 0.9 copy-start.1
  3.4 0.9 copy-start.2

commit v2 on v1

--- a/solution.py
+++ b/solution.py
@@ -19,18 +19,19 @@
 
 def kernel(
     c,
-    routes_ref, gates_ref, tok_ref, cot_ref, wg_hbm, wu_hbm, wd_hbm,
+    routes_hbm, gates_hbm, tok_hbm, cot_hbm, wg_hbm, wu_hbm, wd_hbm,
     dx_ref, dgrad_ref,
-    wg, wu, wd, perm, fin, pcomb,
-    s1, a1, s2, a2, rows, own, st0, rs, gat, keep, pxo, pxi, rt, ra, r2, rc, res,
-    wsem, d1s, d1r, d2s, d2r, cxs, cxr, rss, rsr, ags, agr, pxs, pxr, r1s, r1r, r2s, r2r, fs, fr,
+    routes_ref, gates_ref, tok_ref, cot_ref, wg, wu, wd, perm, fin, pcomb, pad,
+    s1, a1, s2, a2, rows, own, st0, rs, gat, keep, pxo, pxi, rt, rc, res,
+    wsem, d1s, d1r, d2s, d2r, cxs, cxr, rss, rsr, ags, agr, pxs, pxr, hs, hr, fs, fr,
 ):
     n, nz, cap, tok, top, width, hid = c
     half_z = nz // 2
     total = n * n * cap
     chunk = total // nz
     block = n * cap
-    per = nz // n
+    pieces = n * n // nz
+    room = -(-cap // 16) * 16
     hw = width // 2
     hh = hid // 2
     order = [r for pair in zip(range(n // 2, 0, -1), range(n - n // 2, n)) for r in pair]
@@ -43,12 +44,6 @@
     first = (1 - core) * mx + core * my
     second = (1 - core) * my + core * mx
 
-    def at_x(p):
-        return {"expert": p * n + my}
-
-    def at_y(p):
-        return {"expert": mx * n + p}
-
     def at_first(p):
         return {"expert": (1 - core) * (p * n + my) + core * (mx * n + p)}
 
@@ -67,21 +62,28 @@
     mine = span(core, hw)
     theirs = span(1 - core, hw)
 
-    loads = [
+    inputs = [
         pltpu.make_async_copy(src, dst, wsem.at[i])
-        for i, (src, dst) in enumerate(((wg_hbm, wg), (wu_hbm, wu), (wd_hbm, wd)))
+        for i, (src, dst) in enumerate((
+            (routes_hbm, routes_ref), (gates_hbm, gates_ref), (tok_hbm, tok_ref), (cot_hbm, cot_ref),
+            (wg_hbm, wg), (wu_hbm, wu), (wd_hbm, wd),
+        ))
     ]
-    for load in loads:
+    for load in inputs:
         load.start()
-
+    loads = inputs[4:]
+
+    ex = n * n
     barrier = pltpu.get_barrier_semaphore()
-    peers = [at_x(lax.rem(mx + r, n)) for r in range(1, n)]
-    peers += [at_y(lax.rem(my + r, n)) for r in range(1, n)]
-    peers += [other, z_to[0], z_to[1]]
-    for peer in peers:
+
+    def greet(r, _):
+        pl.semaphore_signal(barrier, inc=1, device_id={"expert": lax.rem(me + r, ex)}, device_id_type=MESH)
+        return 0
+
+    lax.fori_loop(1, ex, greet, 0)
+    for peer in (other, z_to[0], z_to[1]):
         pl.semaphore_signal(barrier, inc=1, device_id=peer, device_id_type=MESH)
 
-    ex = n * n
     e_row = lax.broadcasted_iota(jnp.int32, (ex, 1), 0).astype(F32)
     e_div = jnp.floor((e_row + 0.5) * (1.0 / n))
     e_swap = (e_row - e_div * n) * n + e_div
@@ -94,6 +96,8 @@
     earlier = (
         lax.broadcasted_iota(jnp.int32, (tok, tok), 0) < lax.broadcasted_iota(jnp.int32, (tok, tok), 1)
     ).astype(BF16)
+    inputs[0].wait()
+    inputs[1].wait()
     routes = routes_ref[...].astype(F32)
     gates = gates_ref[...].astype(F32)
 
@@ -106,14 +110,15 @@
             weight = weight + jnp.where(hit, gates[k : k + 1, :], 0.0)
         rank = dot(member.astype(BF16), earlier)
         placed = (member * (rank + 1.0)).astype(BF16)
-        return dot(expand, placed) == s_rank + 1.0, weight
-
-    picked, weight = select(e_disp)
+        return placed, weight
+
+    placed, weight = select(e_disp)
+    picked = dot(expand, placed) == s_rank + 1.0
     chosen = jnp.where(picked, 1.0, 0.0).astype(BF16)
-    weighted = jnp.where(picked, dot(expand, weight.astype(BF16)), 0.0).astype(BF16)
+    inputs[2].wait()
     s1[0] = dot(chosen, tok_ref[:, mine]).astype(BF16)
 
-    pl.semaphore_wait(barrier, len(peers))
+    pl.semaphore_wait(barrier, ex + 2)
 
     def exchange(src, dst, ssem, rsem, here, where):
         out = []
@@ -143,19 +148,17 @@
 
     go(d1[0])
     a1[0, span(first, block), :] = s1[0, span(first, block), :]
+
+    s_a = jnp.floor((s_row + 0.5) * (1.0 / block))
+    s_b = s_exp - s_a * n
+    lane = lax.broadcasted_iota(jnp.int32, (total, total), 1).astype(F32)
+    perm[...] = jnp.where(lane == s_b * block + s_a * cap + s_rank, 1.0, 0.0).astype(BF16)
+
+    weighted = jnp.where(picked, dot(expand, weight.astype(BF16)), 0.0).astype(BF16)
+    inputs[3].wait()
     s1[1] = dot(weighted, cot_ref[:, mine]).astype(BF16)
     go(d1[1])
     a1[1, span(first, block), :] = s1[1, span(first, block), :]
-
-    s_a = jnp.floor((s_row + 0.5) * (1.0 / block))
-    s_b = s_exp - s_a * n
-    swapped = s_b * block + s_a * cap + s_rank
-    lane = lax.broadcasted_iota(jnp.int32, (total, total), 1).astype(F32)
-    perm[...] = jnp.where(lane == swapped, 1.0, 0.0).astype(BF16)
-    last = s_row + core_f * (swapped - s_row)
-    fin[...] = jnp.where(lane == last, 1.0, 0.0).astype(BF16)
-    back_home, _ = select(e_row)
-    pcomb[...] = jnp.where(back_home, 1.0, 0.0).astype(BF16)
 
     def stage_two(i):
         for copy in d1[i]:
@@ -177,8 +180,9 @@
     ]
 
     def stage_three(i):
-        for copy in d2[i]:
-            copy.wait_recv()
+        if i:
+            for copy in d2[i]:
+                copy.wait_recv()
         rows[i, :, mine] = dot(fin[...], a2[i]).astype(BF16)
         go([swap[i]])
         swap[i].wait_recv()
@@ -257,6 +261,15 @@
 
     stage_two(0)
     stage_two(1)
+    s_d = jnp.floor((s_exp + 0.5) * (1.0 / pieces))
+    s_x = jnp.floor((s_d + 0.5) * (1.0 / n)) * pieces + (s_exp - s_d * pieces)
+    s_y = s_d + s_x + (mx + my).astype(F32)
+    s_y = s_y - jnp.floor((s_y + 0.5) * (1.0 / n)) * n
+    by_y = s_y * block + s_x * cap + s_rank
+    by_x = s_x * block + s_y * cap + s_rank
+    fin[...] = jnp.where(lane == by_y + core_f * (by_x - by_y), 1.0, 0.0).astype(BF16)
+    for copy in d2[0]:
+        copy.wait_recv()
     stage_three(0)
     partial(0)
     rs_step(0, 0)
@@ -271,7 +284,6 @@
         rs_step(s, 0)
         rs_step(s, 1)
         rs_step(s - 1, 2)
-    rs_step(half_z - 1, 2)
 
     here = span(z, chunk)
     gate = rs_sum(0)
@@ -280,6 +292,7 @@
     up = rs_sum(1)
     gat[2, here, :] = (silu * up).astype(BF16)
     go([ag_copy(d, 0, 2) for d in range(2)])
+    rs_step(half_z - 1, 2)
     back = rs_sum(2)
     gat[0, here, :] = (back * up * sig * (1.0 + gate * (1.0 - sig))).astype(BF16)
     go([ag_copy(d, 0, 0) for d in range(2)])
@@ -299,47 +312,80 @@
         pxo[k] = keep[k, :, theirs].astype(BF16)
         go([px_copy(k)])
 
-    def home_copy(k):
+    def piece(k, p):
         at = z_off(k)
-        peer = at // per
-        sub = lax.rem(at, per)
-        slot = lax.rem(peer + n - my, n) * per + sub
-        return pltpu.make_async_remote_copy(
-            src_ref=rt.at[k], dst_ref=ra.at[span(my * per + sub, chunk), :],
-            send_sem=r1s.at[slot], recv_sem=r1r.at[slot],
-            device_id=at_y(peer), device_id_type=MESH,
+        px = (at // n * pieces if nz > n else 0) + p
+        peer = px * n + lax.rem(at + px + mx + my, n)
+        return peer, pltpu.make_async_remote_copy(
+            src_ref=rt.at[k, span(p, room), :], dst_ref=rc.at[span(me, room), :],
+            send_sem=hs.at[k * pieces + p], recv_sem=hr.at[me],
+            device_id={"expert": peer}, device_id_type=MESH,
         )
 
     def settle(k):
         px_copy(k).wait_recv()
         val = (keep[k, :, mine] + pxi[k].astype(F32)).astype(BF16)
-        rt[k] = val
-        at = z_off(k)
-
-        @pl.when(at // per == my)
-        def _():
-            ra[span(at, chunk), :] = val
-
-        @pl.when(at // per != my)
-        def _():
-            home_copy(k).start()
+        rt[k] = dot(pad[...], val).astype(BF16)
+
+        def send(p, _):
+            peer, copy = piece(k, p)
+
+            @pl.when(peer != me)
+            def _():
+                copy.start()
+
+            @pl.when(peer == me)
+            def _():
+                rc[span(me, room), :] = rt[k, span(p, room), :]
+
+            return 0
+
+        lax.fori_loop(0, pieces, send, 0)
 
     grads(0)
+
+    p_row = lax.broadcasted_iota(jnp.int32, (pieces * room, 1), 0).astype(F32)
+    p_div = jnp.floor((p_row + 0.5) * (1.0 / room))
+    p_rank = p_row - p_div * room
+    p_lane = lax.broadcasted_iota(jnp.int32, (pieces * room, chunk), 1).astype(F32)
+    pad[...] = jnp.where((p_lane == p_div * cap + p_rank) & (p_rank < cap), 1.0, 0.0).astype(BF16)
+    h_row = lax.broadcasted_iota(jnp.int32, (ex * room, 1), 0).astype(F32)
+    h_exp = jnp.floor((h_row + 0.5) * (1.0 / room))
+    h_rank = h_row - h_exp * room
+    unfold = (h_exp == lax.broadcasted_iota(jnp.int32, (ex * room, ex), 1).astype(F32)).astype(BF16)
+    placed, _ = select(e_row)
+    h_hit = (dot(unfold, placed) == h_rank + 1.0) & (h_rank < cap)
+    eye = (
+        lax.broadcasted_iota(jnp.int32, (tok, tok), 0) == lax.broadcasted_iota(jnp.int32, (tok, tok), 1)
+    ).astype(BF16)
+    pcomb[...] = dot(eye, jnp.where(h_hit, 1.0, 0.0).astype(BF16), ((1,), (1,))).astype(BF16)
+
+    def forward(s, j):
+        for d in range(2):
+            ag_arrived(d, s - 1, j)
+            if s < half_z:
+                go([ag_copy(d, s, j)])
+
     done = [0]
-    for s in range(1, half_z + 1):
-        for j in (2, 0, 1):
-            for d in range(2):
-                ag_arrived(d, s - 1, j)
-                if s < half_z:
-                    go([ag_copy(d, s, j)])
-        for k in done:
-            settle(k)
-        done = [s, nz - s] if s < half_z else [s]
-        if s == half_z:
-            grads(s)
-        else:
-            grads(s)
-            grads(nz - s)
+    for s in range(1, half_z):
+        forward(s, 0)
+        settle(done[0])
+        forward(s, 1)
+        grads(s)
+        if len(done) > 1:
+            settle(done[1])
+        forward(s, 2)
+        grads(nz - s)
+        done = [s, nz - s]
+    for k in done:
+        settle(k)
+    forward(half_z, 0)
+    forward(half_z, 1)
+    grads(half_z)
+    settle(half_z)
+
+    for d in range(2):
+        ag_arrived(d, half_z - 1, 2)
     ftile = 256 if hid % 256 == 0 else hid
 
     def down(f, _):
@@ -347,42 +393,45 @@
         dgrad_ref[cols, :] = dot(gat[2, :, cols], rows[1], ((0,), (0,))).astype(BF16)
         return 0
 
-    for k in done:
-        settle(k)
     lax.fori_loop(0, hid // ftile, down, 0)
 
-    for r in range(1, n):
-        for sub in range(per):
-            slot = r * per + sub
+    for copy in pending:
+        copy.wait_send()
+
+    def sent(i, _):
+        k, p = i // pieces, lax.rem(i, pieces)
+        peer, copy = piece(k, p)
+
+        @pl.when(peer != me)
+        def _():
+            copy.wait_send()
+
+        return 0
+
+    lax.fori_loop(0, ex, sent, 0)
+
+    def arrive(e, _):
+        @pl.when(e != me)
+        def _():
             pltpu.make_async_remote_copy(
-                src_ref=rt.at[0],
-                dst_ref=ra.at[span(lax.rem(my + n - r, n) * per + sub, chunk), :],
-                send_sem=r1s.at[slot], recv_sem=r1r.at[slot],
-                device_id=at_y(lax.rem(my + r, n)), device_id_type=MESH,
+                src_ref=rt.at[0, span(0, room), :], dst_ref=rc.at[span(e, room), :],
+                send_sem=hs.at[0], recv_sem=hr.at[e],
+                device_id={"expert": e}, device_id_type=MESH,
             ).wait_recv()
-    r2[...] = dot(perm[...], ra[...]).astype(BF16)
-    home = exchange(r2, rc, r2s, r2r, mx, at_x)
-    go(home)
-    rc[span(mx, block), :] = r2[span(mx, block), :]
-    for copy in home:
-        copy.wait_recv()
-    res[:, mine] = dot(pcomb[...], rc[...], ((0,), (0,))).astype(BF16)
+
+        return 0
+
+    lax.fori_loop(0, ex, arrive, 0)
+    res[:, mine] = dot(pcomb[...], rc[...]).astype(BF16)
     last_swap = pltpu.make_async_remote_copy(
         src_ref=res.at[:, mine], dst_ref=res.at[:, mine], send_sem=fs.at[0], recv_sem=fr.at[0],
         device_id=other, device_id_type=MESH,
     )
-    go([last_swap])
+    last_swap.start()
     last_swap.wait_recv()
     dx_ref[...] = res[...]
 
-    for copy in pending:
-        copy.wait_send()
-    for k in range(nz):
-        at = z_off(k)
-
-        @pl.when(at // per != my)
-        def _():
-            home_copy(k).wait_send()
+    last_swap.wait_send()
 
 
 def body(tokens, cotangent, routes, gates, w_gate, w_up, w_down):
@@ -397,13 +446,17 @@
     chunk = total // nz
     hw = width // 2
     hz = nz // 2
+    pieces = experts // nz
+    room = -(-cap // 16) * 16
     vm = pltpu.VMEM
     dma = pltpu.SemaphoreType.DMA
     in_vmem = pl.BlockSpec(memory_space=pltpu.VMEM)
-    in_hbm = pl.BlockSpec(memory_space=pl.ANY)
+    in_hbm = pl.BlockSpec(memory_space=pltpu.HBM)
     scratch = [
+        vm((top, tok), routes.dtype), vm((top, tok), BF16), vm((tok, width), BF16), vm((tok, width), BF16),
         vm((width, hid), BF16), vm((width, hid), BF16), vm((hid, width), BF16),
-        vm((total, total), BF16), vm((total, total), BF16), vm((total, tok), BF16),
+        vm((total, total), BF16), vm((total, total), BF16), vm((tok, experts * room), BF16),
+        vm((pieces * room, chunk), BF16),
         vm((2, total, hw), BF16), vm((2, total, hw), BF16), vm((2, total, hw), BF16), vm((2, total, hw), BF16),
         vm((2, total, width), BF16),
         vm((3, total, hid), F32),
@@ -411,16 +464,15 @@
         vm((2, hz, 3, chunk, hid), BF16),
         vm((3, total, hid), BF16),
         vm((nz, chunk, width), F32),
-        vm((nz, chunk, hw), BF16), vm((nz, chunk, hw), BF16), vm((nz, chunk, hw), BF16),
-        vm((total, hw), BF16), vm((total, hw), BF16), vm((total, hw), BF16),
+        vm((nz, chunk, hw), BF16), vm((nz, chunk, hw), BF16),
+        vm((nz, pieces * room, hw), BF16), vm((experts * room, hw), BF16),
         vm((tok, width), BF16),
-        dma((3,)),
+        dma((7,)),
         dma((2, n)), dma((2, n)), dma((2, n)), dma((2, n)),
         dma((2,)), dma((2,)),
         dma((2, hz, 3)), dma((2, hz, 3)), dma((2, hz, 3)), dma((2, hz, 3)),
         dma((nz,)), dma((nz,)),
-        dma((nz,)), dma((nz,)),
-        dma((n,)), dma((n,)),
+        dma((experts,)), dma((experts,)),
         dma((1,)), dma((1,)),
     ]
     dx, dgrad = pl.pallas_call(
@@ -429,11 +481,11 @@
             jax.ShapeDtypeStruct((tok, width), BF16),
             jax.ShapeDtypeStruct((hid, width), BF16),
         ),
-        in_specs=[in_vmem] * 4 + [in_hbm] * 3,
+        in_specs=[in_hbm] * 7,
         out_specs=(in_vmem, in_vmem),
         scratch_shapes=scratch,
         compiler_params=pltpu.CompilerParams(
-            collective_id=0, has_side_effects=True, vmem_limit_bytes=52 * 1024 * 1024
+            collective_id=0, has_side_effects=True, vmem_limit_bytes=62 * 1024 * 1024
         ),
         cost_estimate=pl.CostEstimate(
             flops=12 * total * width * hid, bytes_accessed=8 * width * hid, transcendentals=chunk * hid

time: 125 us -> 121 us (0.968)
  the two profiles are of different devices: /device:TPU:65 before, /device:TPU:14 now
where the time goes in v2:
time: 121 us; the launch traced here: 119 us
  Pallas kernels  115 us (95%)
  local copies, waits for them, and re-layouts  3.63 us (3%)
    pallas_call x1, Pallas kernels, body(): pl.pallas_call(functools.partial(kernel, (n, nz, cap, tok, top, width, hi...  115 us
    unnamed x2, local copies, waits for them, and re-layouts  3.63 us

profile of v2, /device:TPU:14, one launch (start us, length us, event | category | flops | bytes accessed | tf_op | source)
XLA Modules:
  0.0 119.2 jit_solution(16006908793146176703)
XLA Ops:
  0.6 114.9 %shard_map.86 = (bf16[128,512]{1,0:T(8,128)(2,1)}, bf16[768,512]{1,0:T(8,128)(2,1)}) custom-call(s32[4,128]{1,0:T(4,128)} %bitcast.10, bf16[4,128]{1,0:T(4,128)(2,1)} %bitcast.11, bf16[128,512]{1,0:T(8,128)(2,1)} %tok_hbm.1, bf16[128,512]{1,0:T(8,128)(2,1)} %cot_hbm.1, bf16[512,768]{1,0:T(8,128)(2,1)} %bitcast.7, bf16[512,768]{1,0:T(8,128)(2,1)} %bitcast.8, ...), custom_call_target="tpu_custom_call" | custom-call | flops 3019898880 | bytes 3145728 | tf_op jit(solution)/shard_map/pallas_call | solution.py:478
  115.5 1.6 %copy.11 = bf16[128,512]{1,0:T(8,128)(2,1)} copy(bf16[128,512]{1,0:T(8,128)(2,1)} %get-tuple-element.8) | data formatting | bytes 262144
  117.1 2.1 %copy.12 = bf16[1,768,512]{2,1,0:T(8,128)(2,1)} copy(bf16[1,768,512]{2,1,0:T(8,128)(2,1)} %bitcast.6) | data formatting | bytes 1572864

commit v3 on v2

--- a/solution.py
+++ b/solution.py
@@ -20,8 +20,8 @@
 def kernel(
     c,
     routes_hbm, gates_hbm, tok_hbm, cot_hbm, wg_hbm, wu_hbm, wd_hbm,
-    dx_ref, dgrad_ref,
-    routes_ref, gates_ref, tok_ref, cot_ref, wg, wu, wd, perm, fin, pcomb, pad,
+    dx_hbm, dgrad_hbm,
+    dgrad_ref, routes_ref, gates_ref, tok_ref, cot_ref, wg, wu, wd, perm, fin, pcomb, pad,
     s1, a1, s2, a2, rows, own, st0, rs, gat, keep, pxo, pxi, rt, rc, res,
     wsem, d1s, d1r, d2s, d2r, cxs, cxr, rss, rsr, ags, agr, pxs, pxr, hs, hr, fs, fr,
 ):
@@ -190,8 +190,6 @@
     tile = 256 if hid % 256 == 0 else hid
 
     def partial(j):
-        loads[j].wait()
-
         def step(f, _):
             cols = span(f, tile)
             if j == 2:
@@ -219,7 +217,12 @@
 
     def rs_step(s, j):
         if s == 0:
-            st0[j] = own[j, span(z_off(half_z), chunk), :].astype(BF16)
+            far = span(z_off(half_z), chunk)
+            loads[j].wait()
+            if j == 2:
+                st0[j] = dot(rows[1, far, :], wd[...], ((1,), (1,))).astype(BF16)
+            else:
+                st0[j] = dot(rows[0, far, :], (wg, wu)[j][...]).astype(BF16)
             go([ring[0, 0, j], ring[1, 0, j]])
             return
         for d in range(2):
@@ -271,15 +274,15 @@
     for copy in d2[0]:
         copy.wait_recv()
     stage_three(0)
+    rs_step(0, 0)
+    rs_step(0, 1)
     partial(0)
-    rs_step(0, 0)
     partial(1)
-    rs_step(0, 1)
     rs_step(1, 0)
     rs_step(1, 1)
     stage_three(1)
+    rs_step(0, 2)
     partial(2)
-    rs_step(0, 2)
     for s in range(2, half_z):
         rs_step(s, 0)
         rs_step(s, 1)
@@ -394,6 +397,8 @@
         return 0
 
     lax.fori_loop(0, hid // ftile, down, 0)
+    store_dgrad = pltpu.make_async_copy(dgrad_ref, dgrad_hbm, wsem.at[0])
+    store_dgrad.start()
 
     for copy in pending:
         copy.wait_send()
@@ -429,9 +434,29 @@
     )
     last_swap.start()
     last_swap.wait_recv()
-    dx_ref[...] = res[...]
+    store_dx = pltpu.make_async_copy(res, dx_hbm, wsem.at[1])
+    store_dx.start()
+    store_dgrad.wait()
+    store_dx.wait()
 
     last_swap.wait_send()
+
+
+def hand_out(dx, dgrad, dx_out, dgrad_out, dx_held, dgrad_held, sems):
+    part = dgrad.shape[0] // 4
+    legs = [(dx, dx_held, dx_out)]
+    for i in range(4):
+        at = pl.ds(i * part, part)
+        legs.append((dgrad.at[at, :], dgrad_held.at[at, :], dgrad_out.at[at, :]))
+    into = [pltpu.make_async_copy(src, held, sems.at[0, i]) for i, (src, held, _) in enumerate(legs)]
+    out = [pltpu.make_async_copy(held, dst, sems.at[1, i]) for i, (_, held, dst) in enumerate(legs)]
+    for copy in into:
+        copy.start()
+    for first, then in zip(into, out):
+        first.wait()
+        then.start()
+    for copy in out:
+        copy.wait()
 
 
 def body(tokens, cotangent, routes, gates, w_gate, w_up, w_down):
@@ -450,9 +475,9 @@
     room = -(-cap // 16) * 16
     vm = pltpu.VMEM
     dma = pltpu.SemaphoreType.DMA
-    in_vmem = pl.BlockSpec(memory_space=pltpu.VMEM)
-    in_hbm = pl.BlockSpec(memory_space=pltpu.HBM)
+    in_hbm = pl.BlockSpec(memory_space=pl.ANY)
     scratch = [
+        vm((hid, width), BF16),
         vm((top, tok), routes.dtype), vm((top, tok), BF16), vm((tok, width), BF16), vm((tok, width), BF16),
         vm((width, hid), BF16), vm((width, hid), BF16), vm((hid, width), BF16),
         vm((total, total), BF16), vm((total, total), BF16), vm((tok, experts * room), BF16),
@@ -482,7 +507,7 @@
             jax.ShapeDtypeStruct((hid, width), BF16),
         ),
         in_specs=[in_hbm] * 7,
-        out_specs=(in_vmem, in_vmem),
+        out_specs=(in_hbm, in_hbm),
         scratch_shapes=scratch,
         compiler_params=pltpu.CompilerParams(
             collective_id=0, has_side_effects=True, vmem_limit_bytes=62 * 1024 * 1024
@@ -491,6 +516,20 @@
             flops=12 * total * width * hid, bytes_accessed=8 * width * hid, transcendentals=chunk * hid
         ),
     )(routes.T, gates.T, tokens, cotangent, w_gate[0], w_up[0], w_down[0])
+    dx, dgrad = pl.pallas_call(
+        hand_out,
+        out_shape=(
+            jax.ShapeDtypeStruct((tok, width), BF16),
+            jax.ShapeDtypeStruct((hid, width), BF16),
+        ),
+        in_specs=[in_hbm] * 2,
+        out_specs=(in_hbm, in_hbm),
+        scratch_shapes=[vm((tok, width), BF16), vm((hid, width), BF16), dma((2, 5))],
+        compiler_params=pltpu.CompilerParams(vmem_limit_bytes=62 * 1024 * 1024),
+        cost_estimate=pl.CostEstimate(
+            flops=0, bytes_accessed=4 * width * (hid + tok), transcendentals=0
+        ),
+    )(dx, dgrad)
     return dx, dgrad[None]
 
 

time: 121 us -> 118 us (0.975)
  local copies, waits for them, and re-layouts: 3.63 us -> 0 us
    unnamed x2 -> x0, local copies, waits for them, and re-layouts: 3.63 us -> none
    pallas_call x0 -> x1, Pallas kernels: none -> 2.01 us  [body(): pl.pallas_call(hand_out, out_shape=(jax.ShapeDtypeStruct((tok, width), BF...]
    pallas_call x1, Pallas kernels: 115 us -> 113 us  [body(): pl.pallas_call(functools.partial(kernel, (n, nz, cap, tok, top, width, hi...]
where the time goes in v3:
time: 118 us; the launch traced here: 116 us
  Pallas kernels  115 us (97%)
    pallas_call x1, Pallas kernels, body(): pl.pallas_call(functools.partial(kernel, (n, nz, cap, tok, top, width, hi...  113 us

profile of v3, /device:TPU:14, one launch (start us, length us, event | category | flops | bytes accessed | tf_op | source)
XLA Modules:
  0.0 116.0 jit_solution(5376912434688529512)
XLA Ops:
  0.6 113.4 %shard_map.86 = (bf16[128,512]{1,0:T(8,128)(2,1)}, bf16[768,512]{1,0:T(8,128)(2,1)}) custom-call(s32[4,128]{1,0:T(4,128)} %bitcast.10, bf16[4,128]{1,0:T(4,128)(2,1)} %bitcast.11, bf16[128,512]{1,0:T(8,128)(2,1)} %tok_hbm.1, bf16[128,512]{1,0:T(8,128)(2,1)} %cot_hbm.1, bf16[512,768]{1,0:T(8,128)(2,1)} %bitcast.6, bf16[512,768]{1,0:T(8,128)(2,1)} %bitcast.7, ...), custom_call_target="tpu_custom_call" | custom-call | flops 3019898880 | bytes 3145728 | tf_op jit(solution)/shard_map/pallas_call | solution.py:503
  114.0 2.0 %shard_map.87 = (bf16[128,512]{1,0:T(8,128)(2,1)}, bf16[768,512]{1,0:T(8,128)(2,1)}) custom-call(bf16[128,512]{1,0:T(8,128)(2,1)} %get-tuple-element.6.dx, bf16[768,512]{1,0:T(8,128)(2,1)} %get-tuple-element.7.dgrad), custom_call_target="tpu_custom_call" | custom-call | bytes 1835008 | tf_op jit(solution)/shard_map/pallas_call | solution.py:519
